TPU v7x, 256 devices: a whole 4x4x8 slice. The times are simulated.
256 devices in a mesh: section: 32 (over y_hi, z, core), ctx: 8 (over y_lo, x).
Axes of the slice: x: 4, y: 4 (y_hi: 2, y_lo: 2; y = y_hi * 2 + y_lo), z: 8, core: 2. Of those that a mesh axis runs over, the one named last changes fastest.
Arguments:
- queries: bfloat16 [32, 1024, 8192], P('section', 'ctx'), may hold values from -6 to 6
- key_states: bfloat16 [32, 1024, 1024], P('section', 'ctx'), may hold values from -6 to 6
- value_states: bfloat16 [32, 1024, 1024], P('section', 'ctx'), may hold values from -1.5 to 1.5
- out_grad: bfloat16 [32, 1024, 8192], P('section', 'ctx'), may hold values from -6 to 6
- node_end: int32 [32, 1024], P('section'), may hold values from 1 to 1024, as said below
- block_list: int32 [32, 8, 8], P('section'), may hold values from 0 to 7, as said below
- block_count: int32 [32, 8], P('section'), may hold values from 1 to 8, as said below
Outputs:
- query_grads: bfloat16 [32, 1024, 8192], P('section', 'ctx')
- key_grads: bfloat16 [32, 1024, 1024], P('section', 'ctx')
- value_grads: bfloat16 [32, 1024, 1024], P('section', 'ctx')
Inputs may be any that keep to these rules, and one draw needn't show every extreme that they name: Each section packs search trees one after another, each in preorder; node_end[s, j] is one past the last node of node j's subtree, so j is an ancestor of i (or i itself) exactly when j <= i < node_end[s, j]. Row b of block_list[s] lists, in increasing order, every key block that holds an ancestor (or the node itself) of some node of query block b, and no other; b itself is always listed; entries after the first block_count[s, b] are 0. block_count[s, b] is the number of listed key blocks of query block b, at most b + 1.
All inputs are finite; a program needn't handle non-finite values.
Results may differ from a plain program's by a relative error of at most 0.0053.
Values may be sent and summed in bfloat16 or wider, within the bound.
No kernel may reach another device: no remote copies, remote signals or barrier semaphores. Data moves between devices by JAX's collectives and lax.ppermute only.
A program may use at most 128 MiB of HBM per device.

v0:
```python
import math
import jax
import jax.numpy as jnp
from jax import lax
from jax.sharding import PartitionSpec as P

HEADS = 64
KV_HEADS = 8
HEAD_DIM = 128
BLK = 128


def from_behind(block, axis, distance):
    devices = range(lax.axis_size(axis))
    route = [((i - distance) % len(devices), i) for i in devices]
    return lax.ppermute(block, axis, route)


def allowed_mask(end_row, list_rows, count_row):
    length = end_row.shape[0]
    block_total = list_rows.shape[0]
    position = jnp.arange(length, dtype=jnp.int32)
    ancestry = (position[None, :] <= position[:, None]) & (position[:, None] < end_row[None, :])
    entries = jnp.arange(block_total, dtype=jnp.int32)
    listed = jnp.any(
        (list_rows[:, :, None] == entries[None, None, :])
        & (entries[None, :, None] < count_row[:, None, None]),
        axis=1,
    )
    spread = jnp.repeat(jnp.repeat(listed, BLK, axis=0), BLK, axis=1)
    return ancestry & spread


def head_block(query_rows, grad_rows, key_rows, value_rows, allowed):
    row_total = query_rows.shape[0]
    scale = 1.0 / math.sqrt(HEAD_DIM)
    query_heads = query_rows.reshape(row_total, -1, HEAD_DIM)
    grad_heads = grad_rows.reshape(row_total, -1, HEAD_DIM)
    scores = (
        jnp.einsum("qhd,kd->hqk", query_heads, key_rows, preferred_element_type=jnp.float32) * scale
    )
    scores = jnp.where(allowed[None], scores, -jnp.inf)
    row_max = jnp.max(scores, axis=2, keepdims=True)
    exponent = jnp.exp(scores - row_max)
    attention = exponent / jnp.sum(exponent, axis=2, keepdims=True)
    attention_half = attention.astype(jnp.bfloat16)
    weight_grad = jnp.einsum(
        "qhd,kd->hqk", grad_heads, value_rows, preferred_element_type=jnp.float32
    )
    row_delta = jnp.sum(attention * weight_grad, axis=2, keepdims=True)
    score_grad = (attention * (weight_grad - row_delta) * scale).astype(jnp.bfloat16)
    query_grad = jnp.einsum(
        "hqk,kd->qhd", score_grad, key_rows, preferred_element_type=jnp.float32
    ).reshape(row_total, -1)
    key_grad = jnp.einsum(
        "hqk,qhd->kd", score_grad, query_heads, preferred_element_type=jnp.float32
    )
    value_grad = jnp.einsum(
        "hqk,qhd->kd", attention_half, grad_heads, preferred_element_type=jnp.float32
    )
    return (query_grad, key_grad, value_grad)


def per_device(queries, key_states, value_states, out_grad, node_end, block_list, block_count):
    node_count = queries.shape[1]
    allowed = allowed_mask(node_end[0], block_list[0], block_count[0])
    ratio = HEADS // KV_HEADS
    full_keys, full_values = (
        lax.all_gather(key_states, "ctx", axis=1, tiled=True),
        lax.all_gather(value_states, "ctx", axis=1, tiled=True),
    )
    length = full_keys.shape[1]
    row_allowed = lax.dynamic_slice_in_dim(
        allowed, lax.axis_index("ctx") * node_count, node_count, 0
    )
    width = ratio * HEAD_DIM

    def per_group(group_index, carry):
        query_acc, pair_acc = carry
        query_grad, key_grad, value_grad = head_block(
            lax.dynamic_slice_in_dim(queries[0], group_index * width, width, 1),
            lax.dynamic_slice_in_dim(out_grad[0], group_index * width, width, 1),
            lax.dynamic_slice_in_dim(full_keys[0], group_index * HEAD_DIM, HEAD_DIM, 1),
            lax.dynamic_slice_in_dim(full_values[0], group_index * HEAD_DIM, HEAD_DIM, 1),
            row_allowed,
        )
        query_acc = lax.dynamic_update_slice_in_dim(
            query_acc, query_grad.astype(jnp.bfloat16), group_index * width, 1
        )
        pair_acc = lax.dynamic_update_slice_in_dim(
            pair_acc, jnp.stack([key_grad, value_grad]), group_index * HEAD_DIM, 2
        )
        return (query_acc, pair_acc)

    start_query = jnp.zeros((node_count, queries.shape[2]), jnp.bfloat16)
    start_pair = jnp.zeros((2, length, key_states.shape[2]), jnp.float32)
    query_acc, pair_acc = lax.fori_loop(0, KV_HEADS, per_group, (start_query, start_pair))
    summed = lax.psum_scatter(pair_acc, "ctx", scatter_dimension=1, tiled=True)
    query_nodes = query_acc[None]
    pair_nodes = summed.astype(jnp.bfloat16)
    query_sent = from_behind(query_nodes, "section", -1)
    pair_sent = from_behind(pair_nodes, "section", -1)
    return (query_sent, pair_sent[0:1], pair_sent[1:2])


def solution(mesh):
    placed = (
        P("section", "ctx", None),
        P("section", "ctx", None),
        P("section", "ctx", None),
        P("section", "ctx", None),
        P("section", None),
        P("section", None, None),
        P("section", None),
    )
    return jax.shard_map(
        per_device,
        mesh=mesh,
        in_specs=placed,
        out_specs=(P("section", "ctx", None), P("section", "ctx", None), P("section", "ctx", None)),
        check_vma=False,
    )
```

profile of v0, /device:TPU:6, one launch (start us, length us, event | category | flops | bytes accessed | tf_op | source)
XLA Modules:
  0.0 464.5 jit_solution(3999073993154204466)
XLA Ops:
  11.5 42.9 %all-gather.3.cloned.1.call-done = bf16[1,1024,1024]{2,1,0:T(8,128)(2,1)} async-done(((bf16[1,128,1024]{2,1,0:T(8,128)(2,1)}), bf16[1,1024,1024]{2,1,0:T(8,128)(2,1)}) %all-gather.3.cloned.1.call-update) | async-done | bytes 2097168 | tf_op jit(solution)/shard_map/all_gather | solution.py:69
  54.4 45.2 %all-gather.5.cloned.1.call-done = bf16[1,1024,1024]{2,1,0:T(8,128)(2,1)} async-done(((bf16[1,128,1024]{2,1,0:T(8,128)(2,1)}), bf16[1,1024,1024]{2,1,0:T(8,128)(2,1)}) %all-gather.5.cloned.1.call-update) | async-done | bytes 2097168 | tf_op jit(solution)/shard_map/all_gather | solution.py:70
  101.1 4.3 broadcast_in_dim.57
  105.4 228.4 %while.15 = (s32[]{:T(128)}, bf16[128,8192]{1,0:T(8,128)(2,1)}, f32[2,1024,1024]{2,1,0:T(8,128)}, bf16[1,1024,1024]{2,1,0:T(8,128)(2,1)}, pred[128,1024]{0,1:T(8...) while((s32[]{:T(128)}, bf16[128,8192]{1,0:T(8,128)(2,1)}, ...), condition=%wide.region_5.6_spmd, body=%wide.region_1.5_spmd.sunk | while | flops 1363547136 | bytes 46289144 | solution.py:97
  110.4 4.3 fusion.88
  114.7 7.1 %fusion.91 = f32[1,1024,128]{2,1,0:T(8,128)S(1)} fusion(bf16[128,8,128]{0,2,1:T(8,128)(2,1)S(1)} %bitcast.121, f32[1024,128,8]{1,0,2:T(8,128)} %fusion.87, f32[8,128,1024]{1,2,0:T(8,128)} %get-tuple-element.238, f32[8,128]{1,0:T(8,128)S(1)} %get-tuple-element.239), kind=kOutput, calls=%fused_computation.19.clone.1 | convolution fusion | flops 275777536 | bytes 9179136 | tf_op jit(solution)/shard_map/while/body/eval_jaxpr/hqk,qhd->kd/dot_general | solution.py:55
  121.7 7.3 %fusion.89 = bf16[128,8,128]{2,0,1:T(8,128)(2,1)S(1)} fusion(f32[1024,128,8]{1,0,2:T(8,128)} %fusion.87, bf16[1,1024,1024]{2,1,0:T(8,128)(2,1)} %get-tuple-element.269, s32[]{:T(128)S(6)} %select_n.45, f32[8,128,1024]{1,2,0:T(8,128)} %get-tuple-element.238, f32[8,128]{1,0:T(8,128)S(1)} %get-tuple-element.239), kind=kOutput, calls=%fused_computation.21.clone.1 | convolution fusion | flops 275908608 | bytes 17309700 | tf_op jit(solution)/shard_map/while/body/eval_jaxpr/hqk,kd->qhd/dot_general | solution.py:52
  139.0 4.3 fusion.88
  143.2 7.1 %fusion.91 = f32[1,1024,128]{2,1,0:T(8,128)S(1)} fusion(bf16[128,8,128]{0,2,1:T(8,128)(2,1)S(1)} %bitcast.121, f32[1024,128,8]{1,0,2:T(8,128)} %fusion.87, f32[8,128,1024]{1,2,0:T(8,128)} %get-tuple-element.238, f32[8,128]{1,0:T(8,128)S(1)} %get-tuple-element.239), kind=kOutput, calls=%fused_computation.19.clone.1 | convolution fusion | flops 275777536 | bytes 9179136 | tf_op jit(solution)/shard_map/while/body/eval_jaxpr/hqk,qhd->kd/dot_general | solution.py:55
  150.3 7.3 %fusion.89 = bf16[128,8,128]{2,0,1:T(8,128)(2,1)S(1)} fusion(f32[1024,128,8]{1,0,2:T(8,128)} %fusion.87, bf16[1,1024,1024]{2,1,0:T(8,128)(2,1)} %get-tuple-element.269, s32[]{:T(128)S(6)} %select_n.45, f32[8,128,1024]{1,2,0:T(8,128)} %get-tuple-element.238, f32[8,128]{1,0:T(8,128)S(1)} %get-tuple-element.239), kind=kOutput, calls=%fused_computation.21.clone.1 | convolution fusion | flops 275908608 | bytes 17309700 | tf_op jit(solution)/shard_map/while/body/eval_jaxpr/hqk,kd->qhd/dot_general | solution.py:52
  167.5 4.2 fusion.88
  171.8 7.1 %fusion.91 = f32[1,1024,128]{2,1,0:T(8,128)S(1)} fusion(bf16[128,8,128]{0,2,1:T(8,128)(2,1)S(1)} %bitcast.121, f32[1024,128,8]{1,0,2:T(8,128)} %fusion.87, f32[8,128,1024]{1,2,0:T(8,128)} %get-tuple-element.238, f32[8,128]{1,0:T(8,128)S(1)} %get-tuple-element.239), kind=kOutput, calls=%fused_computation.19.clone.1 | convolution fusion | flops 275777536 | bytes 9179136 | tf_op jit(solution)/shard_map/while/body/eval_jaxpr/hqk,qhd->kd/dot_general | solution.py:55
  178.9 7.3 %fusion.89 = bf16[128,8,128]{2,0,1:T(8,128)(2,1)S(1)} fusion(f32[1024,128,8]{1,0,2:T(8,128)} %fusion.87, bf16[1,1024,1024]{2,1,0:T(8,128)(2,1)} %get-tuple-element.269, s32[]{:T(128)S(6)} %select_n.45, f32[8,128,1024]{1,2,0:T(8,128)} %get-tuple-element.238, f32[8,128]{1,0:T(8,128)S(1)} %get-tuple-element.239), kind=kOutput, calls=%fused_computation.21.clone.1 | convolution fusion | flops 275908608 | bytes 17309700 | tf_op jit(solution)/shard_map/while/body/eval_jaxpr/hqk,kd->qhd/dot_general | solution.py:52
  196.1 4.3 fusion.88
  200.3 7.1 %fusion.91 = f32[1,1024,128]{2,1,0:T(8,128)S(1)} fusion(bf16[128,8,128]{0,2,1:T(8,128)(2,1)S(1)} %bitcast.121, f32[1024,128,8]{1,0,2:T(8,128)} %fusion.87, f32[8,128,1024]{1,2,0:T(8,128)} %get-tuple-element.238, f32[8,128]{1,0:T(8,128)S(1)} %get-tuple-element.239), kind=kOutput, calls=%fused_computation.19.clone.1 | convolution fusion | flops 275777536 | bytes 9179136 | tf_op jit(solution)/shard_map/while/body/eval_jaxpr/hqk,qhd->kd/dot_general | solution.py:55
  207.4 7.3 %fusion.89 = bf16[128,8,128]{2,0,1:T(8,128)(2,1)S(1)} fusion(f32[1024,128,8]{1,0,2:T(8,128)} %fusion.87, bf16[1,1024,1024]{2,1,0:T(8,128)(2,1)} %get-tuple-element.269, s32[]{:T(128)S(6)} %select_n.45, f32[8,128,1024]{1,2,0:T(8,128)} %get-tuple-element.238, f32[8,128]{1,0:T(8,128)S(1)} %get-tuple-element.239), kind=kOutput, calls=%fused_computation.21.clone.1 | convolution fusion | flops 275908608 | bytes 17309700 | tf_op jit(solution)/shard_map/while/body/eval_jaxpr/hqk,kd->qhd/dot_general | solution.py:52
  221.0 3.6 fusion.87
  224.6 4.3 fusion.88
  228.9 7.1 %fusion.91 = f32[1,1024,128]{2,1,0:T(8,128)S(1)} fusion(bf16[128,8,128]{0,2,1:T(8,128)(2,1)S(1)} %bitcast.121, f32[1024,128,8]{1,0,2:T(8,128)} %fusion.87, f32[8,128,1024]{1,2,0:T(8,128)} %get-tuple-element.238, f32[8,128]{1,0:T(8,128)S(1)} %get-tuple-element.239), kind=kOutput, calls=%fused_computation.19.clone.1 | convolution fusion | flops 275777536 | bytes 9179136 | tf_op jit(solution)/shard_map/while/body/eval_jaxpr/hqk,qhd->kd/dot_general | solution.py:55
  236.0 7.3 %fusion.89 = bf16[128,8,128]{2,0,1:T(8,128)(2,1)S(1)} fusion(f32[1024,128,8]{1,0,2:T(8,128)} %fusion.87, bf16[1,1024,1024]{2,1,0:T(8,128)(2,1)} %get-tuple-element.269, s32[]{:T(128)S(6)} %select_n.45, f32[8,128,1024]{1,2,0:T(8,128)} %get-tuple-element.238, f32[8,128]{1,0:T(8,128)S(1)} %get-tuple-element.239), kind=kOutput, calls=%fused_computation.21.clone.1 | convolution fusion | flops 275908608 | bytes 17309700 | tf_op jit(solution)/shard_map/while/body/eval_jaxpr/hqk,kd->qhd/dot_general | solution.py:52
  253.2 4.3 fusion.88
  257.4 7.1 %fusion.91 = f32[1,1024,128]{2,1,0:T(8,128)S(1)} fusion(bf16[128,8,128]{0,2,1:T(8,128)(2,1)S(1)} %bitcast.121, f32[1024,128,8]{1,0,2:T(8,128)} %fusion.87, f32[8,128,1024]{1,2,0:T(8,128)} %get-tuple-element.238, f32[8,128]{1,0:T(8,128)S(1)} %get-tuple-element.239), kind=kOutput, calls=%fused_computation.19.clone.1 | convolution fusion | flops 275777536 | bytes 9179136 | tf_op jit(solution)/shard_map/while/body/eval_jaxpr/hqk,qhd->kd/dot_general | solution.py:55
  264.5 7.3 %fusion.89 = bf16[128,8,128]{2,0,1:T(8,128)(2,1)S(1)} fusion(f32[1024,128,8]{1,0,2:T(8,128)} %fusion.87, bf16[1,1024,1024]{2,1,0:T(8,128)(2,1)} %get-tuple-element.269, s32[]{:T(128)S(6)} %select_n.45, f32[8,128,1024]{1,2,0:T(8,128)} %get-tuple-element.238, f32[8,128]{1,0:T(8,128)S(1)} %get-tuple-element.239), kind=kOutput, calls=%fused_computation.21.clone.1 | convolution fusion | flops 275908608 | bytes 17309700 | tf_op jit(solution)/shard_map/while/body/eval_jaxpr/hqk,kd->qhd/dot_general | solution.py:52
  281.7 4.3 fusion.88
  286.0 7.1 %fusion.91 = f32[1,1024,128]{2,1,0:T(8,128)S(1)} fusion(bf16[128,8,128]{0,2,1:T(8,128)(2,1)S(1)} %bitcast.121, f32[1024,128,8]{1,0,2:T(8,128)} %fusion.87, f32[8,128,1024]{1,2,0:T(8,128)} %get-tuple-element.238, f32[8,128]{1,0:T(8,128)S(1)} %get-tuple-element.239), kind=kOutput, calls=%fused_computation.19.clone.1 | convolution fusion | flops 275777536 | bytes 9179136 | tf_op jit(solution)/shard_map/while/body/eval_jaxpr/hqk,qhd->kd/dot_general | solution.py:55
  293.0 7.3 %fusion.89 = bf16[128,8,128]{2,0,1:T(8,128)(2,1)S(1)} fusion(f32[1024,128,8]{1,0,2:T(8,128)} %fusion.87, bf16[1,1024,1024]{2,1,0:T(8,128)(2,1)} %get-tuple-element.269, s32[]{:T(128)S(6)} %select_n.45, f32[8,128,1024]{1,2,0:T(8,128)} %get-tuple-element.238, f32[8,128]{1,0:T(8,128)S(1)} %get-tuple-element.239), kind=kOutput, calls=%fused_computation.21.clone.1 | convolution fusion | flops 275908608 | bytes 17309700 | tf_op jit(solution)/shard_map/while/body/eval_jaxpr/hqk,kd->qhd/dot_general | solution.py:52
  310.3 4.3 fusion.88
  314.5 7.1 %fusion.91 = f32[1,1024,128]{2,1,0:T(8,128)S(1)} fusion(bf16[128,8,128]{0,2,1:T(8,128)(2,1)S(1)} %bitcast.121, f32[1024,128,8]{1,0,2:T(8,128)} %fusion.87, f32[8,128,1024]{1,2,0:T(8,128)} %get-tuple-element.238, f32[8,128]{1,0:T(8,128)S(1)} %get-tuple-element.239), kind=kOutput, calls=%fused_computation.19.clone.1 | convolution fusion | flops 275777536 | bytes 9179136 | tf_op jit(solution)/shard_map/while/body/eval_jaxpr/hqk,qhd->kd/dot_general | solution.py:55
  321.6 7.3 %fusion.89 = bf16[128,8,128]{2,0,1:T(8,128)(2,1)S(1)} fusion(f32[1024,128,8]{1,0,2:T(8,128)} %fusion.87, bf16[1,1024,1024]{2,1,0:T(8,128)(2,1)} %get-tuple-element.269, s32[]{:T(128)S(6)} %select_n.45, f32[8,128,1024]{1,2,0:T(8,128)} %get-tuple-element.238, f32[8,128]{1,0:T(8,128)S(1)} %get-tuple-element.239), kind=kOutput, calls=%fused_computation.21.clone.1 | convolution fusion | flops 275908608 | bytes 17309700 | tf_op jit(solution)/shard_map/while/body/eval_jaxpr/hqk,kd->qhd/dot_general | solution.py:52
  337.7 90.9 %reduce-scatter.2.cloned.1.call-done = f32[2,128,1024]{2,1,0:T(8,128)} async-done(((f32[2,1024,1024]{2,1,0:T(8,128)}), f32[2,128,1024]{2,1,0:T(8,128)}) %reduce-scatter.2.cloned.1.call-update) | async-done | bytes 1048592 | tf_op jit(solution)/shard_map/reduce_scatter | solution.py:98
  429.9 17.4 %collective-permute-start.1 = (bf16[2,128,1024]{2,1,0:T(8,128)(2,1)S(1)}, bf16[2,128,1024]{2,1,0:T(8,128)(2,1)S(1)}, u32[]{:S(2)}, u32[]{:S(2)}) collective-permute-start(bf16[2,128,1024]{2,1,0:T(8,128)(2,1)S(1)} %convert_element_type.30), channel_id=1, source_target_pairs={{8,0},{16,8},{24,16},{32,24},{40,32},{48,40},{56,48},{64,56},{72,6... | collective-permute-start | bytes 1572872 | tf_op jit(solution)/shard_map/ppermute | solution.py:16
  447.3 6.7 %collective-permute-done.1 = bf16[2,128,1024]{2,1,0:T(8,128)(2,1)S(1)} collective-permute-done((bf16[2,128,1024]{2,1,0:T(8,128)(2,1)S(1)}, bf16[2,128,1024]{2,1,0:T(8,128)(2,1)S(1)}, u32[]{:S(2)}, u32[]{:S(2)}) %collective-permute-start.1) | collective-permute-done | bytes 524320 | tf_op jit(solution)/shard_map/ppermute | solution.py:16
  (82 shorter events, 90.6 us)
Async XLA Ops:
  7.2 47.2 %all-gather.3.cloned.1.call-start = ((), (), s32[]{:S(2)}) async-start(), calls=%async_computation.1 | async-start | bytes 2359296 | tf_op jit(solution)/shard_map/all_gather | solution.py:69
  7.9 91.6 %all-gather.5.cloned.1.call-start = ((), (), s32[]{:S(2)}) async-start(), calls=%async_computation.2 | async-start | bytes 2359296 | tf_op jit(solution)/shard_map/all_gather | solution.py:70
  8.6 420.0 %reduce-scatter.2.cloned.1.call-start = ((), (), s32[]{:S(2)}) async-start(), calls=%async_computation.3 | async-start | bytes 9437184 | tf_op jit(solution)/shard_map/reduce_scatter | solution.py:98
  333.7 1.6 copy-start
  335.3 112.0 %collective-permute-start = (bf16[1,128,8192]{2,1,0:T(8,128)(2,1)S(1)}, bf16[1,128,8192]{2,1,0:T(8,128)(2,1)}, u32[]{:S(2)}, u32[]{:S(2)}) collective-permute-start(bf16[1,128,8192]{2,1,0:T(8,128)(2,1)S(1)} %bitcast.123), channel_id=1, source_target_pairs={{8,0},{16,8},{24,16},{32,24},{40,32},{48,40},{56,48},{64,56},{72,6... | collective-permute-start | bytes 6291464 | tf_op jit(solution)/shard_map/ppermute | solution.py:16
  429.9 24.1 %collective-permute-start.1 = (bf16[2,128,1024]{2,1,0:T(8,128)(2,1)S(1)}, bf16[2,128,1024]{2,1,0:T(8,128)(2,1)S(1)}, u32[]{:S(2)}, u32[]{:S(2)}) collective-permute-start(bf16[2,128,1024]{2,1,0:T(8,128)(2,1)S(1)} %convert_element_type.30), channel_id=1, source_target_pairs={{8,0},{16,8},{24,16},{32,24},{40,32},{48,40},{56,48},{64,56},{72,6... | collective-permute-start | bytes 1572872 | tf_op jit(solution)/shard_map/ppermute | solution.py:16
Sparse Core Ops, SparseCore 0:
  9.8 44.5 all-gather.2
  56.2 43.3 all-gather.4
  333.9 94.7 reduce-scatter.1
where the time goes:
time: 466 us; the launch traced here: 464 us
  matrix products  201 us (43%)
  waiting for transfers between devices  187 us (40%)
  local copies, waits for them, and re-layouts  29.9 us (6%)
  starting transfers between devices  19.9 us (4%)
  between operations  13.8 us (3%)
  other arithmetic  12.6 us (3%)
    reduce_scatter x1, waiting for transfers between devices, per_device(): summed = lax.psum_scatter(pair_acc, 'ctx', scatter_dimension=1, tiled=True)  90.9 us
    dot_general x8, matrix products, head_block(): jnp.einsum('hqk,kd->qhd', score_grad, key_rows, preferred_element_type=jn...  58.1 us
    dot_general x8, matrix products, head_block(): jnp.einsum('hqk,qhd->kd', score_grad, query_heads, preferred_element_type...  56.6 us
    all_gather x1, waiting for transfers between devices, per_device(): lax.all_gather(value_states, 'ctx', axis=1, tiled=True)  45.2 us
    all_gather x1, waiting for transfers between devices, per_device(): lax.all_gather(key_states, 'ctx', axis=1, tiled=True)  42.9 us
    sub x8, matrix products, head_block(): exponent = jnp.exp(scores - row_max)  34 us
    dot_general x8, matrix products, head_block(): jnp.einsum('qhd,kd->hqk', grad_heads, value_rows, preferred_element_type=...  29 us
    dot_general x8, matrix products, head_block(): jnp.einsum('hqk,qhd->kd', attention_half, grad_heads, preferred_element_t...  23.1 us
  transfers between devices with their start and end apart: 5, of which 4 were waited for; matrix products, arithmetic and copies ran while one was open for 1% of the time, Pallas kernels for 0%

commit v1 on v0

--- a/solution.py
+++ b/solution.py
@@ -62,11 +62,18 @@
 
 
 def per_device(queries, key_states, value_states, out_grad, node_end, block_list, block_count):
+
+    def carry_limits(comm_axis, state):
+        o_now = tuple((state for _ in range(lax.axis_size(comm_axis))))
+        back = jnp.stack(o_now, axis=0)
+        outer = lax.all_to_all(back, comm_axis, 0, 0)
+        return jnp.concatenate(outer, axis=1)
+
     node_count = queries.shape[1]
     allowed = allowed_mask(node_end[0], block_list[0], block_count[0])
     ratio = HEADS // KV_HEADS
     full_keys, full_values = (
-        lax.all_gather(key_states, "ctx", axis=1, tiled=True),
+        carry_limits("ctx", key_states),
         lax.all_gather(value_states, "ctx", axis=1, tiled=True),
     )
     length = full_keys.shape[1]

time: 466 us -> 438 us (0.940)
  waiting for transfers between devices: 187 us -> 146 us
  starting transfers between devices: 19.9 us -> 32.6 us
    all_gather x1 -> x0, waiting for transfers between devices: 42.9 us -> none  [per_device(): lax.all_gather(key_states, 'ctx', axis=1, tiled=True)]
    all_to_all x0 -> x1, waiting for transfers between devices: none -> 36.1 us  [carry_limits(): outer = lax.all_to_all(back, comm_axis, 0, 0)]
    all_gather x1, waiting for transfers between devices: 45.2 us -> 11.8 us  [per_device(): lax.all_gather(value_states, 'ctx', axis=1, tiled=True)]
    all_to_all x0 -> x1, starting transfers between devices: none -> 6.45 us  [carry_limits(): outer = lax.all_to_all(back, comm_axis, 0, 0)]
    ppermute x2, starting transfers between devices: 19.8 us -> 26.2 us  [from_behind(): return lax.ppermute(block, axis, route)]
where the time goes in v1:
time: 438 us; the launch traced here: 437 us
  matrix products  201 us (46%)
  waiting for transfers between devices  146 us (33%)
  starting transfers between devices  32.6 us (7%)
  local copies, waits for them, and re-layouts  32.4 us (7%)
  between operations  14.1 us (3%)
  other arithmetic  10.6 us (2%)
    reduce_scatter x1, waiting for transfers between devices, per_device(): summed = lax.psum_scatter(pair_acc, 'ctx', scatter_dimension=1, tiled=True)  90.6 us
    dot_general x8, matrix products, head_block(): jnp.einsum('hqk,kd->qhd', score_grad, key_rows, preferred_element_type=jn...  58.1 us
    dot_general x8, matrix products, head_block(): jnp.einsum('hqk,qhd->kd', score_grad, query_heads, preferred_element_type...  56.6 us
    all_to_all x1, waiting for transfers between devices, carry_limits(): outer = lax.all_to_all(back, comm_axis, 0, 0)  36.1 us
    sub x8, matrix products, head_block(): exponent = jnp.exp(scores - row_max)  34 us
    dot_general x8, matrix products, head_block(): jnp.einsum('qhd,kd->hqk', grad_heads, value_rows, preferred_element_type=...  29 us
    ppermute x2, starting transfers between devices, from_behind(): return lax.ppermute(block, axis, route)  26.2 us
    dot_general x8, matrix products, head_block(): jnp.einsum('hqk,qhd->kd', attention_half, grad_heads, preferred_element_t...  23.1 us
  transfers between devices with their start and end apart: 5, of which 4 were waited for; matrix products, arithmetic and copies ran while one was open for 1% of the time, Pallas kernels for 0%

profile of v1, /device:TPU:6, one launch (start us, length us, event | category | flops | bytes accessed | tf_op | source)
XLA Modules:
  0.0 436.8 jit_solution(13315281609352339937)
XLA Ops:
  10.5 6.5 %all-to-all-start = ((bf16[8,1,128,1024]{3,2,1,0:T(8,128)(2,1)}), bf16[8,1,128,1024]{3,2,1,0:T(8,128)(2,1)}, u32[]{:S(2)}, u32[]{:S(2)}) async-start(bf16[8,1,128,1024]{3,2,1,0:T(8,128)(2,1)} %stack.32), calls=%async_computation | async-start | bytes 4194304 | tf_op jit(solution)/shard_map/all_to_all | solution.py:69
  17.7 36.1 %all-to-all-done = bf16[8,1,128,1024]{3,2,1,0:T(8,128)(2,1)} async-done(((bf16[8,1,128,1024]{3,2,1,0:T(8,128)(2,1)}), bf16[8,1,128,1024]{3,2,1,0:T(8,128)(2,1)}, u32[]{:S(2)}, u32[]{:S(2)}) %all-to-all-start) | async-done | bytes 2097184 | tf_op jit(solution)/shard_map/all_to_all | solution.py:69
  53.8 11.8 %all-gather.2.cloned.1.call-done = bf16[1,1024,1024]{2,1,0:T(8,128)(2,1)} async-done(((bf16[1,128,1024]{2,1,0:T(8,128)(2,1)}), bf16[1,1024,1024]{2,1,0:T(8,128)(2,1)}) %all-gather.2.cloned.1.call-update) | async-done | bytes 2097168 | tf_op jit(solution)/shard_map/all_gather | solution.py:77
  67.1 4.3 broadcast_in_dim.57
  71.4 228.3 %while.15 = (s32[]{:T(128)}, bf16[128,8192]{1,0:T(8,128)(2,1)}, f32[2,1024,1024]{2,1,0:T(8,128)}, bf16[8,1,128,1024]{3,2,0,1:T(8,128)(2,1)}, pred[128,1024]{0,1:...) while((s32[]{:T(128)}, bf16[128,8192]{1,0:T(8,128)(2,1)}, ...), condition=%wide.region_5.6_spmd, body=%wide.region_1.5_spmd.sunk | while | flops 1363547136 | bytes 46289144 | solution.py:104
  76.5 4.2 fusion.88
  80.7 7.1 %fusion.91 = f32[1,1024,128]{2,1,0:T(8,128)S(1)} fusion(bf16[128,8,128]{0,2,1:T(8,128)(2,1)S(1)} %bitcast.124, f32[1024,128,8]{1,0,2:T(8,128)} %fusion.87, f32[8,128,1024]{1,2,0:T(8,128)} %get-tuple-element.246, f32[8,128]{1,0:T(8,128)S(1)} %get-tuple-element.247), kind=kOutput, calls=%fused_computation.19.clone.1 | convolution fusion | flops 275777536 | bytes 9179136 | tf_op jit(solution)/shard_map/while/body/eval_jaxpr/hqk,qhd->kd/dot_general | solution.py:55
  87.8 7.3 %fusion.89 = bf16[128,8,128]{2,0,1:T(8,128)(2,1)S(1)} fusion(f32[1024,128,8]{1,0,2:T(8,128)} %fusion.87, bf16[1024,1024]{1,0:T(8,128)(2,1)} %bitcast.118, s32[]{:T(128)S(6)} %select_n.45, f32[8,128,1024]{1,2,0:T(8,128)} %get-tuple-element.246, f32[8,128]{1,0:T(8,128)S(1)} %get-tuple-element.247), kind=kOutput, calls=%fused_computation.21.clone.1 | convolution fusion | flops 275908608 | bytes 17309700 | tf_op jit(solution)/shard_map/while/body/eval_jaxpr/hqk,kd->qhd/dot_general | solution.py:52
  105.0 4.2 fusion.88
  109.2 7.1 %fusion.91 = f32[1,1024,128]{2,1,0:T(8,128)S(1)} fusion(bf16[128,8,128]{0,2,1:T(8,128)(2,1)S(1)} %bitcast.124, f32[1024,128,8]{1,0,2:T(8,128)} %fusion.87, f32[8,128,1024]{1,2,0:T(8,128)} %get-tuple-element.246, f32[8,128]{1,0:T(8,128)S(1)} %get-tuple-element.247), kind=kOutput, calls=%fused_computation.19.clone.1 | convolution fusion | flops 275777536 | bytes 9179136 | tf_op jit(solution)/shard_map/while/body/eval_jaxpr/hqk,qhd->kd/dot_general | solution.py:55
  116.3 7.3 %fusion.89 = bf16[128,8,128]{2,0,1:T(8,128)(2,1)S(1)} fusion(f32[1024,128,8]{1,0,2:T(8,128)} %fusion.87, bf16[1024,1024]{1,0:T(8,128)(2,1)} %bitcast.118, s32[]{:T(128)S(6)} %select_n.45, f32[8,128,1024]{1,2,0:T(8,128)} %get-tuple-element.246, f32[8,128]{1,0:T(8,128)S(1)} %get-tuple-element.247), kind=kOutput, calls=%fused_computation.21.clone.1 | convolution fusion | flops 275908608 | bytes 17309700 | tf_op jit(solution)/shard_map/while/body/eval_jaxpr/hqk,kd->qhd/dot_general | solution.py:52
  133.5 4.2 fusion.88
  137.8 7.1 %fusion.91 = f32[1,1024,128]{2,1,0:T(8,128)S(1)} fusion(bf16[128,8,128]{0,2,1:T(8,128)(2,1)S(1)} %bitcast.124, f32[1024,128,8]{1,0,2:T(8,128)} %fusion.87, f32[8,128,1024]{1,2,0:T(8,128)} %get-tuple-element.246, f32[8,128]{1,0:T(8,128)S(1)} %get-tuple-element.247), kind=kOutput, calls=%fused_computation.19.clone.1 | convolution fusion | flops 275777536 | bytes 9179136 | tf_op jit(solution)/shard_map/while/body/eval_jaxpr/hqk,qhd->kd/dot_general | solution.py:55
  144.8 7.3 %fusion.89 = bf16[128,8,128]{2,0,1:T(8,128)(2,1)S(1)} fusion(f32[1024,128,8]{1,0,2:T(8,128)} %fusion.87, bf16[1024,1024]{1,0:T(8,128)(2,1)} %bitcast.118, s32[]{:T(128)S(6)} %select_n.45, f32[8,128,1024]{1,2,0:T(8,128)} %get-tuple-element.246, f32[8,128]{1,0:T(8,128)S(1)} %get-tuple-element.247), kind=kOutput, calls=%fused_computation.21.clone.1 | convolution fusion | flops 275908608 | bytes 17309700 | tf_op jit(solution)/shard_map/while/body/eval_jaxpr/hqk,kd->qhd/dot_general | solution.py:52
  166.3 7.1 %fusion.91 = f32[1,1024,128]{2,1,0:T(8,128)S(1)} fusion(bf16[128,8,128]{0,2,1:T(8,128)(2,1)S(1)} %bitcast.124, f32[1024,128,8]{1,0,2:T(8,128)} %fusion.87, f32[8,128,1024]{1,2,0:T(8,128)} %get-tuple-element.246, f32[8,128]{1,0:T(8,128)S(1)} %get-tuple-element.247), kind=kOutput, calls=%fused_computation.19.clone.1 | convolution fusion | flops 275777536 | bytes 9179136 | tf_op jit(solution)/shard_map/while/body/eval_jaxpr/hqk,qhd->kd/dot_general | solution.py:55
  173.4 7.3 %fusion.89 = bf16[128,8,128]{2,0,1:T(8,128)(2,1)S(1)} fusion(f32[1024,128,8]{1,0,2:T(8,128)} %fusion.87, bf16[1024,1024]{1,0:T(8,128)(2,1)} %bitcast.118, s32[]{:T(128)S(6)} %select_n.45, f32[8,128,1024]{1,2,0:T(8,128)} %get-tuple-element.246, f32[8,128]{1,0:T(8,128)S(1)} %get-tuple-element.247), kind=kOutput, calls=%fused_computation.21.clone.1 | convolution fusion | flops 275908608 | bytes 17309700 | tf_op jit(solution)/shard_map/while/body/eval_jaxpr/hqk,kd->qhd/dot_general | solution.py:52
  190.6 4.2 fusion.88
  194.8 7.1 %fusion.91 = f32[1,1024,128]{2,1,0:T(8,128)S(1)} fusion(bf16[128,8,128]{0,2,1:T(8,128)(2,1)S(1)} %bitcast.124, f32[1024,128,8]{1,0,2:T(8,128)} %fusion.87, f32[8,128,1024]{1,2,0:T(8,128)} %get-tuple-element.246, f32[8,128]{1,0:T(8,128)S(1)} %get-tuple-element.247), kind=kOutput, calls=%fused_computation.19.clone.1 | convolution fusion | flops 275777536 | bytes 9179136 | tf_op jit(solution)/shard_map/while/body/eval_jaxpr/hqk,qhd->kd/dot_general | solution.py:55
  201.9 7.3 %fusion.89 = bf16[128,8,128]{2,0,1:T(8,128)(2,1)S(1)} fusion(f32[1024,128,8]{1,0,2:T(8,128)} %fusion.87, bf16[1024,1024]{1,0:T(8,128)(2,1)} %bitcast.118, s32[]{:T(128)S(6)} %select_n.45, f32[8,128,1024]{1,2,0:T(8,128)} %get-tuple-element.246, f32[8,128]{1,0:T(8,128)S(1)} %get-tuple-element.247), kind=kOutput, calls=%fused_computation.21.clone.1 | convolution fusion | flops 275908608 | bytes 17309700 | tf_op jit(solution)/shard_map/while/body/eval_jaxpr/hqk,kd->qhd/dot_general | solution.py:52
  219.2 4.2 fusion.88
  223.4 7.1 %fusion.91 = f32[1,1024,128]{2,1,0:T(8,128)S(1)} fusion(bf16[128,8,128]{0,2,1:T(8,128)(2,1)S(1)} %bitcast.124, f32[1024,128,8]{1,0,2:T(8,128)} %fusion.87, f32[8,128,1024]{1,2,0:T(8,128)} %get-tuple-element.246, f32[8,128]{1,0:T(8,128)S(1)} %get-tuple-element.247), kind=kOutput, calls=%fused_computation.19.clone.1 | convolution fusion | flops 275777536 | bytes 9179136 | tf_op jit(solution)/shard_map/while/body/eval_jaxpr/hqk,qhd->kd/dot_general | solution.py:55
  230.5 7.3 %fusion.89 = bf16[128,8,128]{2,0,1:T(8,128)(2,1)S(1)} fusion(f32[1024,128,8]{1,0,2:T(8,128)} %fusion.87, bf16[1024,1024]{1,0:T(8,128)(2,1)} %bitcast.118, s32[]{:T(128)S(6)} %select_n.45, f32[8,128,1024]{1,2,0:T(8,128)} %get-tuple-element.246, f32[8,128]{1,0:T(8,128)S(1)} %get-tuple-element.247), kind=kOutput, calls=%fused_computation.21.clone.1 | convolution fusion | flops 275908608 | bytes 17309700 | tf_op jit(solution)/shard_map/while/body/eval_jaxpr/hqk,kd->qhd/dot_general | solution.py:52
  247.7 4.2 fusion.88
  252.0 7.1 %fusion.91 = f32[1,1024,128]{2,1,0:T(8,128)S(1)} fusion(bf16[128,8,128]{0,2,1:T(8,128)(2,1)S(1)} %bitcast.124, f32[1024,128,8]{1,0,2:T(8,128)} %fusion.87, f32[8,128,1024]{1,2,0:T(8,128)} %get-tuple-element.246, f32[8,128]{1,0:T(8,128)S(1)} %get-tuple-element.247), kind=kOutput, calls=%fused_computation.19.clone.1 | convolution fusion | flops 275777536 | bytes 9179136 | tf_op jit(solution)/shard_map/while/body/eval_jaxpr/hqk,qhd->kd/dot_general | solution.py:55
  259.0 7.3 %fusion.89 = bf16[128,8,128]{2,0,1:T(8,128)(2,1)S(1)} fusion(f32[1024,128,8]{1,0,2:T(8,128)} %fusion.87, bf16[1024,1024]{1,0:T(8,128)(2,1)} %bitcast.118, s32[]{:T(128)S(6)} %select_n.45, f32[8,128,1024]{1,2,0:T(8,128)} %get-tuple-element.246, f32[8,128]{1,0:T(8,128)S(1)} %get-tuple-element.247), kind=kOutput, calls=%fused_computation.21.clone.1 | convolution fusion | flops 275908608 | bytes 17309700 | tf_op jit(solution)/shard_map/while/body/eval_jaxpr/hqk,kd->qhd/dot_general | solution.py:52
  276.2 4.2 fusion.88
  280.5 7.1 %fusion.91 = f32[1,1024,128]{2,1,0:T(8,128)S(1)} fusion(bf16[128,8,128]{0,2,1:T(8,128)(2,1)S(1)} %bitcast.124, f32[1024,128,8]{1,0,2:T(8,128)} %fusion.87, f32[8,128,1024]{1,2,0:T(8,128)} %get-tuple-element.246, f32[8,128]{1,0:T(8,128)S(1)} %get-tuple-element.247), kind=kOutput, calls=%fused_computation.19.clone.1 | convolution fusion | flops 275777536 | bytes 9179136 | tf_op jit(solution)/shard_map/while/body/eval_jaxpr/hqk,qhd->kd/dot_general | solution.py:55
  287.6 7.3 %fusion.89 = bf16[128,8,128]{2,0,1:T(8,128)(2,1)S(1)} fusion(f32[1024,128,8]{1,0,2:T(8,128)} %fusion.87, bf16[1024,1024]{1,0:T(8,128)(2,1)} %bitcast.118, s32[]{:T(128)S(6)} %select_n.45, f32[8,128,1024]{1,2,0:T(8,128)} %get-tuple-element.246, f32[8,128]{1,0:T(8,128)S(1)} %get-tuple-element.247), kind=kOutput, calls=%fused_computation.21.clone.1 | convolution fusion | flops 275908608 | bytes 17309700 | tf_op jit(solution)/shard_map/while/body/eval_jaxpr/hqk,kd->qhd/dot_general | solution.py:52
  301.3 8.0 %collective-permute-start = (bf16[1,128,8192]{2,1,0:T(8,128)(2,1)S(1)}, bf16[1,128,8192]{2,1,0:T(8,128)(2,1)}, u32[]{:S(2)}, u32[]{:S(2)}) collective-permute-start(bf16[1,128,8192]{2,1,0:T(8,128)(2,1)S(1)} %bitcast.126), channel_id=1, source_target_pairs={{8,0},{16,8},{24,16},{32,24},{40,32},{48,40},{56,48},{64,56},{72,6... | collective-permute-start | bytes 6291464 | tf_op jit(solution)/shard_map/ppermute | solution.py:16
  309.3 90.6 %reduce-scatter.2.cloned.1.call-done = f32[2,128,1024]{2,1,0:T(8,128)} async-done(((f32[2,1024,1024]{2,1,0:T(8,128)}), f32[2,128,1024]{2,1,0:T(8,128)}) %reduce-scatter.2.cloned.1.call-update) | async-done | bytes 1048592 | tf_op jit(solution)/shard_map/reduce_scatter | solution.py:105
  401.2 18.1 %collective-permute-start.1 = (bf16[2,128,1024]{2,1,0:T(8,128)(2,1)S(1)}, bf16[2,128,1024]{2,1,0:T(8,128)(2,1)S(1)}, u32[]{:S(2)}, u32[]{:S(2)}) collective-permute-start(bf16[2,128,1024]{2,1,0:T(8,128)(2,1)S(1)} %convert_element_type.30), channel_id=1, source_target_pairs={{8,0},{16,8},{24,16},{32,24},{40,32},{48,40},{56,48},{64,56},{72,6... | collective-permute-start | bytes 1572872 | tf_op jit(solution)/shard_map/ppermute | solution.py:16
  419.4 6.7 %collective-permute-done.1 = bf16[2,128,1024]{2,1,0:T(8,128)(2,1)S(1)} collective-permute-done((bf16[2,128,1024]{2,1,0:T(8,128)(2,1)S(1)}, bf16[2,128,1024]{2,1,0:T(8,128)(2,1)S(1)}, u32[]{:S(2)}, u32[]{:S(2)}) %collective-permute-start.1) | collective-permute-done | bytes 524320 | tf_op jit(solution)/shard_map/ppermute | solution.py:16
  (88 shorter events, 95.9 us)
Async XLA Ops:
  7.2 9.8 %copy-start.3 = (s32[1,8]{1,0:T(1,128)S(1)}, s32[1,8]{1,0:T(1,128)}, u32[]{:S(2)}) copy-start(s32[1,8]{1,0:T(1,128)} %param.15) | copy-start | bytes 100
  7.2 9.8 %copy-start.2 = (s32[1,8,8]{2,1,0:T(8,128)S(1)}, s32[1,8,8]{2,1,0:T(8,128)}, u32[]{:S(2)}) copy-start(s32[1,8,8]{2,1,0:T(8,128)} %param.14) | copy-start | bytes 772
  7.2 10.3 %copy-start.1 = (s32[1,1024]{1,0:T(1,128)S(1)}, s32[1,1024]{1,0:T(1,128)}, u32[]{:S(2)}) copy-start(s32[1,1024]{1,0:T(1,128)} %param.13) | copy-start | bytes 12292
  7.2 58.4 %all-gather.2.cloned.1.call-start = ((), (), s32[]{:S(2)}) async-start(), calls=%async_computation.2 | async-start | bytes 2359296 | tf_op jit(solution)/shard_map/all_gather | solution.py:77
  10.5 43.3 %all-to-all-start = ((bf16[8,1,128,1024]{3,2,1,0:T(8,128)(2,1)}), bf16[8,1,128,1024]{3,2,1,0:T(8,128)(2,1)}, u32[]{:S(2)}, u32[]{:S(2)}) async-start(bf16[8,1,128,1024]{3,2,1,0:T(8,128)(2,1)} %stack.32), calls=%async_computation | async-start | bytes 4194304 | tf_op jit(solution)/shard_map/all_to_all | solution.py:69
  16.9 383.0 %reduce-scatter.2.cloned.1.call-start = ((), (), s32[]{:S(2)}) async-start(), calls=%async_computation.3 | async-start | bytes 9437184 | tf_op jit(solution)/shard_map/reduce_scatter | solution.py:105
  299.7 1.6 copy-start
  301.3 118.0 %collective-permute-start = (bf16[1,128,8192]{2,1,0:T(8,128)(2,1)S(1)}, bf16[1,128,8192]{2,1,0:T(8,128)(2,1)}, u32[]{:S(2)}, u32[]{:S(2)}) collective-permute-start(bf16[1,128,8192]{2,1,0:T(8,128)(2,1)S(1)} %bitcast.126), channel_id=1, source_target_pairs={{8,0},{16,8},{24,16},{32,24},{40,32},{48,40},{56,48},{64,56},{72,6... | collective-permute-start | bytes 6291464 | tf_op jit(solution)/shard_map/ppermute | solution.py:16
  401.2 24.8 %collective-permute-start.1 = (bf16[2,128,1024]{2,1,0:T(8,128)(2,1)S(1)}, bf16[2,128,1024]{2,1,0:T(8,128)(2,1)S(1)}, u32[]{:S(2)}, u32[]{:S(2)}) collective-permute-start(bf16[2,128,1024]{2,1,0:T(8,128)(2,1)S(1)} %convert_element_type.30), channel_id=1, source_target_pairs={{8,0},{16,8},{24,16},{32,24},{40,32},{48,40},{56,48},{64,56},{72,6... | collective-permute-start | bytes 1572872 | tf_op jit(solution)/shard_map/ppermute | solution.py:16
Sparse Core Ops, SparseCore 0:
  9.8 55.7 all-gather.1
  299.9 99.9 reduce-scatter.1
